TPU v7x, 128 devices: a whole 4x4x4 slice. The times are simulated.
128 devices in a mesh: dom: 4 (over x), head: 32 (over z, y, core).
Axes of the slice: x: 4, y: 4, z: 4, core: 2. Of those that a mesh axis runs over, the one named last changes fastest.
Arguments:
- tokens: bfloat16 [24, 64, 8192], P(None, 'dom', 'head'), may hold values from -6 to 6
- parents: int32 [64], replicated, may hold values from 0 to 63, as said below
- recurrent_state: float32 [64, 128, 64, 256], P('dom', 'head'), may hold values from -6 to 6
- value_history: float32 [64, 3, 8192], P('dom', None, 'head'), may hold values from -6 to 6
- mixing_history: float32 [64, 3, 2048], P('dom', None, 'head'), may hold values from -6 to 6
- input_gain: float32 [8192], P('head'), may hold values from 0.5 to 1.5
- gate_value_weight: bfloat16 [8192, 2, 8192], P(None, None, 'head'), may hold values from -0.0625 to 0.0625
- mixing_weight: bfloat16 [8192, 2048], P(None, 'head'), may hold values from -0.0625 to 0.0625
- step_weight: bfloat16 [8192, 128], P(None, 'head'), may hold values from -0.0625 to 0.0625
- value_kernel: float32 [4, 8192], P(None, 'head'), may hold values from -3 to 3
- value_offset: float32 [8192], P('head'), may hold values from -0.5 to 0.5
- mixing_kernel: float32 [4, 2048], P(None, 'head'), may hold values from -3 to 3
- mixing_offset: float32 [2048], P('head'), may hold values from -0.5 to 0.5
- step_offset: float32 [128], P('head'), may hold values from -4 to 0
- decay_log: float32 [128], P('head'), may hold values from -2 to 1.5
- skip_gain: float32 [128], P('head'), may hold values from 0.5 to 1.5
- output_gain: float32 [8192], P('head'), may hold values from 0.5 to 1.5
- output_weight: bfloat16 [8192, 8192], P('head'), may hold values from -0.0625 to 0.0625
Outputs:
- mixed: bfloat16 [24, 64, 8192], P(None, 'dom', 'head')
Inputs may be any that keep to these rules, and one draw needn't show every extreme that they name: parents comes from systematic resampling: it never falls with i, and offspring counts are very uneven, so that a particle's parent may sit several blocks of 16 particles away.
All inputs are finite; a program needn't handle non-finite values.
Results may differ from a plain program's by a relative error of at most 0.023.
Values may be sent and summed in bfloat16 or wider, within the bound.
A program may use at most 128 MiB of HBM per device.

v0:
```python
import jax
import jax.numpy as jnp
from jax import lax
from jax.sharding import PartitionSpec as P

STEPS = 24
LP = 16
ROWS = STEPS * LP
GROUPS = 4
LANES = 256
F32 = jnp.float32
BF16 = jnp.bfloat16


def silu(v):
    return v / (1.0 + jnp.exp(-v))


def conv_rows(window, kernel, bias):
    total = bias
    for k in range(4):
        total = total + kernel[k : k + 1] * window[k * LP : k * LP + ROWS]
    return silu(total)


def picked(hot, hist):
    return [jnp.dot(hot, hist[j], preferred_element_type=F32) for j in range(3)]


def body(
    tokens,
    parents,
    state,
    vhist,
    mhist,
    gain,
    gvw,
    mw,
    sw,
    vk,
    vo,
    mk,
    mo,
    so,
    dlog,
    skip,
    ogain,
    ow,
):
    d = lax.axis_index("dom")
    g = lax.axis_index("head") // 8
    full = lax.all_gather(tokens.reshape(ROWS, LANES), "head", axis=1, tiled=True)
    fgain = lax.all_gather(gain.astype(BF16), "head", axis=0, tiled=True).astype(F32)
    xf = full.astype(F32)
    inv = lax.rsqrt(jnp.mean(xf * xf, axis=-1, keepdims=True) + 1e-05)
    normed = (xf * inv * fgain).astype(BF16)
    gate = jnp.dot(normed, gvw[:, 0, :], preferred_element_type=F32)
    value = jnp.dot(normed, gvw[:, 1, :], preferred_element_type=F32)
    mixing = jnp.dot(normed, mw, preferred_element_type=F32)
    step_in = jnp.dot(normed, sw, preferred_element_type=F32)
    own = lax.dynamic_slice_in_dim(parents, d * LP, LP)
    hot = (own[:, None] == jnp.arange(64)[None, :]).astype(BF16)
    vall = lax.all_gather(jnp.moveaxis(vhist, 1, 0).astype(BF16), "dom", axis=1, tiled=True)
    mall = lax.all_gather(jnp.moveaxis(mhist, 1, 0).astype(BF16), "dom", axis=1, tiled=True)
    vact = conv_rows(jnp.concatenate(picked(hot, vall) + [value], 0), vk, vo[None])
    mact = conv_rows(jnp.concatenate(picked(hot, mall) + [mixing], 0), mk, mo[None])
    mixall = lax.all_gather(mact.astype(BF16), "head", axis=1, tiled=True)
    b = lax.dynamic_slice_in_dim(mixall, g * 256, 256, 1)
    c = lax.dynamic_slice_in_dim(mixall, (GROUPS + g) * 256, 256, 1)
    call = lax.all_gather(c, "dom", axis=0, tiled=False)
    sb = state.astype(BF16).reshape(LP, LANES, 256)
    row_parent = jnp.tile(parents.reshape(4, 1, LP), (1, STEPS, 1)).reshape(4 * ROWS)
    lhs = call.reshape(4 * ROWS, 256)
    u = jnp.zeros((4 * ROWS, LANES), F32)
    for q in range(LP):
        mask = (row_parent == d * LP + q).astype(BF16)[:, None]
        u = u + lax.dot_general(
            lhs * mask, sb[q], (((1,), (1,)), ((), ())), preferred_element_type=F32
        )
    from_state = lax.psum_scatter(
        u.astype(BF16).reshape(4, ROWS, LANES), "dom", scatter_dimension=0, tiled=True
    )[0].astype(F32)
    step = jax.nn.softplus(step_in + so[None])
    logdecay = -step * jnp.exp(dlog)[None]
    run = logdecay
    for sh in (1, 2, 4, 8, 16):
        z = jnp.zeros((sh * LP, 4), F32)
        run = run + jnp.concatenate([z, run[: ROWS - sh * LP]], 0)
    gram = lax.dot_general(c, b, (((1,), (1,)), ((), ())), preferred_element_type=F32)
    ri = lax.broadcasted_iota(jnp.int32, (ROWS, ROWS), 0)
    ci = lax.broadcasted_iota(jnp.int32, (ROWS, ROWS), 1)
    keep = (ri % LP == ci % LP) & (ci <= ri)
    gated = []
    for h in range(4):
        col = slice(64 * h, 64 * h + 64)
        diff = jnp.where(keep, run[:, h : h + 1] - run[:, h][None, :], -1e30)
        m = (gram * jnp.exp(diff)).astype(BF16)
        sv = (vact[:, col] * step[:, h : h + 1]).astype(BF16)
        y = jnp.dot(m, sv, preferred_element_type=F32)
        y = y + jnp.exp(run[:, h : h + 1]) * from_state[:, col]
        gated.append(y + skip[h] * vact[:, col])
    gated = jnp.concatenate(gated, 1) * silu(gate)
    sq = jnp.sum(gated * gated, axis=1)
    total = lax.psum(jnp.where(jnp.arange(GROUPS)[:, None] == g, sq[None, :], 0.0), "head")
    total = jnp.sum(jnp.where(jnp.arange(GROUPS)[:, None] == g, total, 0.0), axis=0)
    inv2 = lax.rsqrt(total / 2048.0 + 1e-05)[:, None]
    scaled = (gated * inv2 * ogain[None]).astype(BF16)
    terms = jnp.dot(scaled, ow, preferred_element_type=F32).astype(BF16)
    out = lax.psum_scatter(terms, "head", scatter_dimension=1, tiled=True)
    return out.reshape(STEPS, LP, LANES)


def solution(mesh):
    return jax.shard_map(
        body,
        mesh=mesh,
        in_specs=(
            P(None, "dom", "head"),
            P(),
            P("dom", "head", None, None),
            P("dom", None, "head"),
            P("dom", None, "head"),
            P("head"),
            P(None, None, "head"),
            P(None, "head"),
            P(None, "head"),
            P(None, "head"),
            P("head"),
            P(None, "head"),
            P("head"),
            P("head"),
            P("head"),
            P("head"),
            P("head"),
            P("head", None),
        ),
        out_specs=P(None, "dom", "head"),
        check_vma=False,
    )
```

profile of v0, /device:TPU:0, one launch (start us, length us, event | category | flops | bytes accessed | tf_op | source)
XLA Modules:
  0.0 366.3 jit_solution(3251294010593405401)
XLA Ops:
  6.5 0.7 all-gather.5.cloned.1.call-update
  7.3 0.7 convert_element_type.297
  8.0 25.7 %all-gather.1 = bf16[32,1,256]{2,1,0:T(2,128)(2,1)S(1)} all-gather(bf16[1,1,256]{2,1,0:T(2,128)(2,1)S(1)} %reshape.451), channel_id=1, replica_groups=mesh['dom'=4,'head'=32] {'head'}, dimensions={0}, use_global_device_ids=true | all-gather | bytes 16896 | tf_op jit(solution)/shard_map/all_gather | solution.py:53
  34.4 0.7 dynamic_slice.9
  37.4 0.7 convert_element_type.338
  38.2 0.7 convert_element_type.335
  39.0 0.7 convert_element_type.332
  40.5 0.7 convert_element_type.326
  41.3 0.7 convert_element_type.323
  42.1 0.7 convert_element_type.320
  42.9 0.7 convert_element_type.317
  43.7 0.7 convert_element_type.314
  44.4 0.7 convert_element_type.311
  45.2 0.7 convert_element_type.307
  45.9 2.6 convert_element_type.308
  49.0 12.2 %all_gather.21 = bf16[3,64,64]{2,1,0:T(8,128)(2,1)S(1)} all-gather(bf16[3,16,64]{2,1,0:T(8,128)(2,1)S(1)} %convert_bitcast_fusion.1), channel_id=1, replica_groups=mesh['dom'=4,'head'=32] {'dom'}, dimensions={1}, use_global_device_ids=true | all-gather | bytes 30720 | tf_op jit(solution)/shard_map/all_gather | solution.py:64
  61.3 11.9 %all_gather.25 = bf16[3,64,256]{2,1,0:T(8,128)(2,1)S(1)} all-gather(bf16[3,16,256]{2,1,0:T(8,128)(2,1)S(1)} %convert_bitcast_fusion), channel_id=1, replica_groups=mesh['dom'=4,'head'=32] {'dom'}, dimensions={1}, use_global_device_ids=true | all-gather | bytes 122880 | tf_op jit(solution)/shard_map/all_gather | solution.py:63
  76.8 0.8 fusion.52
  77.6 0.8 fusion.53
  78.4 0.8 fusion.54
  79.2 0.9 fusion.49
  80.1 0.9 fusion.50
  81.0 0.9 fusion.51
  81.8 1.2 fusion.75
  83.0 4.3 %fusion = f32[384]{0:T(512)S(1)} fusion(bf16[384,8192]{1,0:T(8,128)(2,1)} %all-gather.5.cloned.1.call-done), kind=kLoop, calls=%fused_computation.2 | loop fusion | flops 9436800 | bytes 6292992 | tf_op jit(solution)/shard_map/reduce_sum | solution.py:55
  87.6 2.9 fusion.2
  90.6 2.1 fusion.78
  93.2 0.9 divide_convert_fusion
  94.2 17.6 %fusion.74 = (bf16[8192,1,256]{2,1,0:T(2,128)(2,1)}, bf16[8192,1,256]{2,1,0:T(2,128)(2,1)}) fusion(bf16[8192,2,256]{2,1,0:T(2,128)(2,1)} %param.24), kind=kLoop, calls=%fused_computation.198 | loop fusion | bytes 16777216 | tf_op jit(solution)/shard_map/slice | solution.py:57
  111.9 1.8 negate_multiply_fusion
  114.0 22.3 %all-gather.7.cloned.1.call-done = bf16[384,2048]{0,1:T(8,128)(2,1)} async-done(((bf16[384,64]{0,1:T(8,128)(2,1)}), bf16[384,2048]{0,1:T(8,128)(2,1)}) %all-gather.7.cloned.1.call-update) | async-done | bytes 1572880 | tf_op jit(solution)/shard_map/all_gather | solution.py:67
  136.3 0.9 constant_dynamic-slice_fusion
  137.2 14.9 %all-gather = bf16[1536,256]{0,1:T(8,128)(2,1)S(1)} all-gather(bf16[384,256]{0,1:T(8,128)(2,1)S(1)} %constant_dynamic-slice_fusion), channel_id=2, replica_groups=mesh['dom'=4,'head'=32] {'dom'}, dimensions={0}, use_global_device_ids=true | all-gather | bytes 983040 | tf_op jit(solution)/shard_map/all_gather | solution.py:70
  152.6 1.6 broadcast_multiply_fusion
  168.9 1.2 copy.74
  170.6 7.8 %fusion.4 = f32[384,256]{0,1:T(8,128)S(1)} fusion(bf16[384,8192]{1,0:T(8,128)(2,1)} %copy-done.2, bf16[8192,1,256]{2,1,0:T(2,128)(2,1)} %get-tuple-element.18), kind=kOutput, calls=%fused_computation.9 | convolution fusion | flops 1610612736 | bytes 10878976 | tf_op jit(solution)/shard_map/dot_general | solution.py:58
  178.5 0.8 add_divide_fusion
  179.2 1.2 fusion.32
  180.4 10.9 %reduce-scatter.3.cloned.1.call-done = bf16[1,384,256]{1,2,0:T(8,128)(2,1)} async-done(((bf16[4,384,256]{1,2,0:T(8,128)(2,1)}), bf16[1,384,256]{1,2,0:T(8,128)(2,1)}) %reduce-scatter.3.cloned.1.call-update) | async-done | bytes 196624 | tf_op jit(solution)/shard_map/reduce_scatter | solution.py:80
  191.3 1.0 bitcast_convert_fusion
  192.3 1.0 fusion.9
  193.3 1.1 fusion.8
  194.4 1.0 fusion.7
  195.5 1.1 fusion.6
  196.6 7.7 %multiply_reduce_fusion = (f32[384]{0:T(512)S(1)}, f32[384,256]{0,1:T(8,128)S(1)}) fusion(bf16[384,8192]{1,0:T(8,128)(2,1)} %copy-done.2, bf16[8192,1,256]{2,1,0:T(2,128)(2,1)} %get-tuple-element.17, f32[384,64]{0,1:T(8,128)S(1)} %fusion.6, f32[384,64]{0,1:T(8,128)S(1)} %fusion.7, f32[384,64]{0,1:T(8,128)S(1)} %fusion.8, f32[384,64]{0,1:T(8,128)S(1)} %fusion.9), kind=kOutput, calls=%fused_computation.57 | convolution fusion | flops 1611497088 | bytes 11273728 | tf_op jit(solution)/shard_map/dot_general | solution.py:57
  204.4 67.2 %psum.7 = f32[4,384]{1,0:T(4,128)S(1)} all-reduce(f32[4,384]{1,0:T(4,128)S(1)} %broadcast_select_fusion), channel_id=1, replica_groups=mesh['dom'=4,'head'=32] {'head'}, use_global_device_ids=true, to_apply=%region_3.4 | all-reduce | flops 1536 | bytes 12288 | tf_op jit(solution)/shard_map/psum | solution.py:104
  271.6 6.7 %convolution_convert_fusion = bf16[384,8192]{1,0:T(8,128)(2,1)} fusion(bf16[256,8192]{1,0:T(8,128)(2,1)} %param.35, f32[384,256]{0,1:T(8,128)S(1)} %get-tuple-element.82, f32[256]{0:T(256)S(1)} %copy-done.41, f32[384]{0:T(512)S(1)} %add_rsqrt_fusion), kind=kOutput, calls=%fused_computation.5 | convolution fusion | flops 1614053376 | bytes 10881536 | tf_op jit(solution)/shard_map/dot_general | solution.py:108
  278.4 81.4 %reduce-scatter.5.cloned.1.call-done = bf16[384,256]{1,0:T(8,128)(2,1)} async-done(((bf16[384,8192]{1,0:T(8,128)(2,1)}), bf16[384,256]{1,0:T(8,128)(2,1)}) %reduce-scatter.5.cloned.1.call-update) | async-done | bytes 196624 | tf_op jit(solution)/shard_map/reduce_scatter | solution.py:109
  (244 shorter events, 25.2 us)
Async XLA Ops:
  6.5 83.9 %copy-start = (bf16[8192,64]{0,1:T(8,128)(2,1)S(1)}, bf16[8192,64]{0,1:T(8,128)(2,1)}, u32[]{:S(2)}) copy-start(bf16[8192,64]{0,1:T(8,128)(2,1)} %param.25) | copy-start | bytes 3145732
  6.5 76.5 %all-gather.5.cloned.1.call-start = ((), (), s32[]{:S(2)}) async-start(), calls=%async_computation.2 | async-start | bytes 6488064 | tf_op jit(solution)/shard_map/all_gather | solution.py:52
  7.3 129.0 %all-gather.7.cloned.1.call-start = ((), (), s32[]{:S(2)}) async-start(), calls=%async_computation.3 | async-start | bytes 1622016 | tf_op jit(solution)/shard_map/all_gather | solution.py:67
  45.9 3.1 copy-start.28
  45.9 15.4 %copy-start.22 = (f32[16,3,256]{2,0,1:T(8,128)S(1)}, f32[16,3,256]{2,0,1:T(8,128)}, u32[]{:S(2)}) copy-start(f32[16,3,256]{2,0,1:T(8,128)} %param.21) | copy-start | bytes 147460
  45.9 29.0 %copy-start.42 = (f32[4]{0:T(128)S(1)}, f32[4]{0:T(128)}, u32[]{:S(2)}) copy-start(f32[4]{0:T(128)} %param.33) | copy-start | bytes 52
  45.9 29.7 %copy-start.55 = (f32[4,64]{1,0:T(4,128)S(1)}, f32[4,64]{1,0:T(4,128)}, u32[]{:S(2)}) copy-start(f32[4,64]{1,0:T(4,128)} %param.29) | copy-start | bytes 3076
  45.9 30.3 %copy-start.45 = (f32[4,256]{1,0:T(4,128)S(1)}, f32[4,256]{1,0:T(4,128)}, u32[]{:S(2)}) copy-start(f32[4,256]{1,0:T(4,128)} %param.27) | copy-start | bytes 12292
  83.0 4.6 %copy-start.4 = (bf16[384,8192]{1,0:T(8,128)(2,1)S(1)}, bf16[384,8192]{1,0:T(8,128)(2,1)}, u32[]{:S(2)}) copy-start(bf16[384,8192]{1,0:T(8,128)(2,1)} %all-gather.5.cloned.1.call-done) | copy-start | bytes 18874372
  90.5 2.7 copy-start.2
  90.5 2.7 copy-start.25
  90.5 2.7 copy-start.26
  90.5 2.7 copy-start.27
  90.5 2.7 copy-start.50
  90.5 2.7 copy-start.51
  94.1 17.7 %copy-start.21 = (bf16[8192,4]{0,1:T(4,128)(2,1)S(1)}, bf16[8192,4]{0,1:T(4,128)(2,1)}, u32[]{:S(2)}) copy-start(bf16[8192,4]{0,1:T(4,128)(2,1)} %param.26) | copy-start | bytes 196612
  94.1 17.7 %copy-start.43 = (f32[4]{0:T(128)S(1)}, f32[4]{0:T(128)}, u32[]{:S(2)}) copy-start(f32[4]{0:T(128)} %param.31) | copy-start | bytes 52
  94.1 17.7 %copy-start.44 = (f32[4]{0:T(128)S(1)}, f32[4]{0:T(128)}, u32[]{:S(2)}) copy-start(f32[4]{0:T(128)} %exp.42) | copy-start | bytes 52
  94.2 97.2 %reduce-scatter.3.cloned.1.call-start = ((), (), s32[]{:S(2)}) async-start(), calls=%async_computation.4 | async-start | bytes 983040 | tf_op jit(solution)/shard_map/reduce_scatter | solution.py:80
  94.2 17.7 %copy-start.3 = (bf16[384,8192]{1,0:T(8,128)(2,1)S(1)}, bf16[384,8192]{1,0:T(8,128)(2,1)}, u32[]{:S(2)}) copy-start(bf16[384,8192]{1,0:T(8,128)(2,1)} %copy-done.2) | copy-start | bytes 18874372
  113.6 38.7 %copy-start.29 = (bf16[4,384]{1,0:T(4,128)(2,1)S(1)}, bf16[4,384]{1,0:T(4,128)(2,1)}, u32[]{:S(2)}) copy-start(bf16[4,384]{1,0:T(4,128)(2,1)} %convert_element_type.341) | copy-start | bytes 9220
  113.7 38.7 %copy-start.30 = (bf16[4,384]{1,0:T(4,128)(2,1)S(1)}, bf16[4,384]{1,0:T(4,128)(2,1)}, u32[]{:S(2)}) copy-start(bf16[4,384]{1,0:T(4,128)(2,1)} %convert_element_type.338) | copy-start | bytes 9220
  113.7 38.7 %copy-start.31 = (bf16[4,384]{1,0:T(4,128)(2,1)S(1)}, bf16[4,384]{1,0:T(4,128)(2,1)}, u32[]{:S(2)}) copy-start(bf16[4,384]{1,0:T(4,128)(2,1)} %convert_element_type.335) | copy-start | bytes 9220
  113.7 38.8 %copy-start.32 = (bf16[4,384]{1,0:T(4,128)(2,1)S(1)}, bf16[4,384]{1,0:T(4,128)(2,1)}, u32[]{:S(2)}) copy-start(bf16[4,384]{1,0:T(4,128)(2,1)} %convert_element_type.332) | copy-start | bytes 9220
  113.7 38.8 %copy-start.33 = (bf16[4,384]{1,0:T(4,128)(2,1)S(1)}, bf16[4,384]{1,0:T(4,128)(2,1)}, u32[]{:S(2)}) copy-start(bf16[4,384]{1,0:T(4,128)(2,1)} %convert_element_type.329) | copy-start | bytes 9220
  113.7 38.8 %copy-start.34 = (bf16[4,384]{1,0:T(4,128)(2,1)S(1)}, bf16[4,384]{1,0:T(4,128)(2,1)}, u32[]{:S(2)}) copy-start(bf16[4,384]{1,0:T(4,128)(2,1)} %convert_element_type.326) | copy-start | bytes 9220
  113.7 38.8 %copy-start.35 = (bf16[4,384]{1,0:T(4,128)(2,1)S(1)}, bf16[4,384]{1,0:T(4,128)(2,1)}, u32[]{:S(2)}) copy-start(bf16[4,384]{1,0:T(4,128)(2,1)} %convert_element_type.323) | copy-start | bytes 9220
  113.7 38.8 %copy-start.36 = (bf16[4,384]{1,0:T(4,128)(2,1)S(1)}, bf16[4,384]{1,0:T(4,128)(2,1)}, u32[]{:S(2)}) copy-start(bf16[4,384]{1,0:T(4,128)(2,1)} %convert_element_type.320) | copy-start | bytes 9220
  113.7 38.8 %copy-start.37 = (bf16[4,384]{1,0:T(4,128)(2,1)S(1)}, bf16[4,384]{1,0:T(4,128)(2,1)}, u32[]{:S(2)}) copy-start(bf16[4,384]{1,0:T(4,128)(2,1)} %convert_element_type.317) | copy-start | bytes 9220
  113.8 38.8 %copy-start.38 = (bf16[4,384]{1,0:T(4,128)(2,1)S(1)}, bf16[4,384]{1,0:T(4,128)(2,1)}, u32[]{:S(2)}) copy-start(bf16[4,384]{1,0:T(4,128)(2,1)} %convert_element_type.314) | copy-start | bytes 9220
  113.8 38.8 %copy-start.39 = (bf16[4,384]{1,0:T(4,128)(2,1)S(1)}, bf16[4,384]{1,0:T(4,128)(2,1)}, u32[]{:S(2)}) copy-start(bf16[4,384]{1,0:T(4,128)(2,1)} %convert_element_type.311) | copy-start | bytes 9220
  113.9 38.7 %copy-start.40 = (bf16[4,384]{1,0:T(4,128)(2,1)S(1)}, bf16[4,384]{1,0:T(4,128)(2,1)}, u32[]{:S(2)}) copy-start(bf16[4,384]{1,0:T(4,128)(2,1)} %convert_element_type.307) | copy-start | bytes 9220
  114.0 40.3 %copy-start.23 = (f32[384,4]{0,1:T(4,128)}, f32[384,4]{0,1:T(4,128)S(1)}, u32[]{:S(2)}) copy-start(f32[384,4]{0,1:T(4,128)S(1)} %pad_add_fusion.2) | copy-start | bytes 18436
  170.1 189.7 %reduce-scatter.5.cloned.1.call-start = ((), (), s32[]{:S(2)}) async-start(), calls=%async_computation.5 | async-start | bytes 6488064 | tf_op jit(solution)/shard_map/reduce_scatter | solution.py:109
  170.5 7.9 %copy-start.18 = (f32[16,256]{0,1:T(8,128)S(1)}, f32[16,256]{0,1:T(8,128)}, u32[]{:S(2)}) copy-start(f32[16,256]{0,1:T(8,128)} %fusion.49) | copy-start | bytes 49156
  170.5 7.9 %copy-start.19 = (f32[16,256]{0,1:T(8,128)S(1)}, f32[16,256]{0,1:T(8,128)}, u32[]{:S(2)}) copy-start(f32[16,256]{0,1:T(8,128)} %fusion.50) | copy-start | bytes 49156
  170.5 7.9 %copy-start.20 = (f32[16,256]{0,1:T(8,128)S(1)}, f32[16,256]{0,1:T(8,128)}, u32[]{:S(2)}) copy-start(f32[16,256]{0,1:T(8,128)} %fusion.51) | copy-start | bytes 49156
  170.5 7.9 %copy-start.46 = (f32[1,256]{1,0:T(1,128)S(1)}, f32[1,256]{1,0:T(1,128)}, u32[]{:S(2)}) copy-start(f32[1,256]{1,0:T(1,128)} %get-tuple-element.51) | copy-start | bytes 3076
  170.5 7.9 %copy-start.47 = (f32[1,256]{1,0:T(1,128)S(1)}, f32[1,256]{1,0:T(1,128)}, u32[]{:S(2)}) copy-start(f32[1,256]{1,0:T(1,128)} %get-tuple-element.52) | copy-start | bytes 3076
  170.5 7.9 %copy-start.48 = (f32[1,256]{1,0:T(1,128)S(1)}, f32[1,256]{1,0:T(1,128)}, u32[]{:S(2)}) copy-start(f32[1,256]{1,0:T(1,128)} %get-tuple-element.53) | copy-start | bytes 3076
  170.5 7.9 %copy-start.49 = (f32[1,256]{1,0:T(1,128)S(1)}, f32[1,256]{1,0:T(1,128)}, u32[]{:S(2)}) copy-start(f32[1,256]{1,0:T(1,128)} %get-tuple-element.54) | copy-start | bytes 3076
  170.5 7.9 %copy-start.58 = (f32[256]{0:T(256)S(1)}, f32[256]{0:T(256)}, u32[]{:S(2)}) copy-start(f32[256]{0:T(256)} %param.28) | copy-start | bytes 3076
  178.3 13.9 %copy-start.56 = (s32[384]{0:T(512)S(1)}, s32[384]{0:T(512)}, u32[]{:S(2)}) copy-start(s32[384]{0:T(512)} %get-tuple-element.83) | copy-start | bytes 4612
  178.4 13.9 %copy-start.57 = (s32[384]{0:T(512)S(1)}, s32[384]{0:T(512)}, u32[]{:S(2)}) copy-start(s32[384]{0:T(512)} %get-tuple-element.84) | copy-start | bytes 4612
  178.4 13.9 %copy-start.61 = (pred[384]{0:T(512)(128)(4,1)S(1)}, pred[384]{0:T(512)(128)(4,1)}, u32[]{:S(2)}) copy-start(pred[384]{0:T(512)(128)(4,1)} %fusion.64) | copy-start | bytes 1156
  196.6 7.7 %copy-start.54 = (pred[4]{0:T(512)(128)(4,1)S(1)}, pred[4]{0:T(512)(128)(4,1)}, u32[]{:S(2)}) copy-start(pred[4]{0:T(512)(128)(4,1)} %iota_compare_fusion.8) | copy-start | bytes 16
  196.6 75.0 %copy-start.41 = (f32[256]{0:T(256)S(1)}, f32[256]{0:T(256)}, u32[]{:S(2)}) copy-start(f32[256]{0:T(256)} %param.34) | copy-start | bytes 3076
  278.4 81.4 %copy-start.1 = (bf16[8192,64]{0,1:T(8,128)(2,1)S(1)}, bf16[8192,64]{0,1:T(8,128)(2,1)}, u32[]{:S(2)}) copy-start(bf16[8192,64]{0,1:T(8,128)(2,1)} %param.25) | copy-start | bytes 3145732
  (19 other events, 25.5 us)
Sparse Core Ops, SparseCore 0:
  9.5 56.9 all-gather.4
  94.2 41.9 all-gather.6
  170.2 21.0 reduce-scatter.2
  278.5 81.1 reduce-scatter.4
where the time goes:
time: 367 us; the launch traced here: 366 us
  blocking collectives  132 us (36%)
  waiting for transfers between devices  115 us (31%)
  local copies, waits for them, and re-layouts  43.2 us (12%)
  matrix products  43.2 us (12%)
  other arithmetic  18 us (5%)
  between operations  14.3 us (4%)
    reduce_scatter x1, waiting for transfers between devices, body(): out = lax.psum_scatter(terms, 'head', scatter_dimension=1, tiled=True)  81.4 us
    psum x1, blocking collectives, body(): lax.psum(jnp.where(jnp.arange(GROUPS)[:, None] == g, sq[None, :], 0.0), '...  67.2 us
    all_gather x1, blocking collectives, body(): lax.all_gather(gain.astype(BF16), 'head', axis=0, tiled=True).astype(F32)  25.7 us
    all_gather x1, waiting for transfers between devices, body(): mixall = lax.all_gather(mact.astype(BF16), 'head', axis=1, tiled=True)  22.3 us
    slice x1, local copies, waits for them, and re-layouts, body(): gate = jnp.dot(normed, gvw[:, 0, :], preferred_element_type=F32)  17.6 us
    all_gather x1, blocking collectives, body(): call = lax.all_gather(c, 'dom', axis=0, tiled=False)  14.9 us
    all_gather x1, blocking collectives, body(): lax.all_gather(jnp.moveaxis(mhist, 1, 0).astype(BF16), 'dom', axis=1, til...  12.2 us
    all_gather x1, blocking collectives, body(): lax.all_gather(jnp.moveaxis(vhist, 1, 0).astype(BF16), 'dom', axis=1, til...  11.9 us
  transfers between devices with their start and end apart: 4, of which 3 were waited for; matrix products, arithmetic and copies ran while one was open for 15% of the time, Pallas kernels for 0%

commit v1 on v0

--- a/solution.py
+++ b/solution.py
@@ -101,7 +101,10 @@
         gated.append(y + skip[h] * vact[:, col])
     gated = jnp.concatenate(gated, 1) * silu(gate)
     sq = jnp.sum(gated * gated, axis=1)
-    total = lax.psum(jnp.where(jnp.arange(GROUPS)[:, None] == g, sq[None, :], 0.0), "head")
+    total = jnp.sum(
+        lax.all_gather(jnp.where(jnp.arange(GROUPS)[:, None] == g, sq[None, :], 0.0), "head"),
+        axis=0,
+    )
     total = jnp.sum(jnp.where(jnp.arange(GROUPS)[:, None] == g, total, 0.0), axis=0)
     inv2 = lax.rsqrt(total / 2048.0 + 1e-05)[:, None]
     scaled = (gated * inv2 * ogain[None]).astype(BF16)

time: 367 us -> 328 us (0.89)
  blocking collectives: 132 us -> 89.7 us
    psum x1 -> x0, blocking collectives: 67.2 us -> none  [body(): lax.psum(jnp.where(jnp.arange(GROUPS)[:, None] == g, sq[None, :], 0.0), '...]
    all_gather x0 -> x1, blocking collectives: none -> 24.9 us  [body(): lax.all_gather(jnp.where(jnp.arange(GROUPS)[:, None] == g, sq[None, :], 0...]
  transfers between devices with their start and end apart: 4 -> 4, of which waited for: 3 -> 3; matrix products, arithmetic and copies ran while one was open for 15% -> 17% of each run, Pallas kernels for 0% -> 0%
where the time goes in v1:
time: 328 us; the launch traced here: 327 us
  waiting for transfers between devices  118 us (36%)
  blocking collectives  89.7 us (27%)
  local copies, waits for them, and re-layouts  43.2 us (13%)
  matrix products  43.2 us (13%)
  other arithmetic  18.1 us (6%)
  between operations  14.3 us (4%)
    reduce_scatter x1, waiting for transfers between devices, body(): out = lax.psum_scatter(terms, 'head', scatter_dimension=1, tiled=True)  84.1 us
    all_gather x1, blocking collectives, body(): lax.all_gather(gain.astype(BF16), 'head', axis=0, tiled=True).astype(F32)  25.7 us
    all_gather x1, blocking collectives, body(): lax.all_gather(jnp.where(jnp.arange(GROUPS)[:, None] == g, sq[None, :], 0...  24.9 us
    all_gather x1, waiting for transfers between devices, body(): mixall = lax.all_gather(mact.astype(BF16), 'head', axis=1, tiled=True)  22.3 us
    slice x1, local copies, waits for them, and re-layouts, body(): gate = jnp.dot(normed, gvw[:, 0, :], preferred_element_type=F32)  17.6 us
    all_gather x1, blocking collectives, body(): call = lax.all_gather(c, 'dom', axis=0, tiled=False)  14.9 us
    all_gather x1, blocking collectives, body(): lax.all_gather(jnp.moveaxis(mhist, 1, 0).astype(BF16), 'dom', axis=1, til...  12.2 us
    all_gather x1, blocking collectives, body(): lax.all_gather(jnp.moveaxis(vhist, 1, 0).astype(BF16), 'dom', axis=1, til...  11.9 us
  transfers between devices with their start and end apart: 4, of which 3 were waited for; matrix products, arithmetic and copies ran while one was open for 17% of the time, Pallas kernels for 0%

profile of v1, /device:TPU:0, one launch (start us, length us, event | category | flops | bytes accessed | tf_op | source)
XLA Modules:
  0.0 326.9 jit_solution(15188000180892727815)
XLA Ops:
  6.5 0.7 all-gather.5.cloned.1.call-update
  7.3 0.7 convert_element_type.297
  8.0 25.7 %all-gather.1 = bf16[32,1,256]{2,1,0:T(2,128)(2,1)S(1)} all-gather(bf16[1,1,256]{2,1,0:T(2,128)(2,1)S(1)} %reshape.494), channel_id=1, replica_groups=mesh['dom'=4,'head'=32] {'head'}, dimensions={0}, use_global_device_ids=true | all-gather | bytes 16896 | tf_op jit(solution)/shard_map/all_gather | solution.py:53
  34.4 0.7 dynamic_slice.9
  37.4 0.7 convert_element_type.338
  38.2 0.7 convert_element_type.335
  39.0 0.7 convert_element_type.332
  40.5 0.7 convert_element_type.326
  41.3 0.7 convert_element_type.323
  42.1 0.7 convert_element_type.320
  42.9 0.7 convert_element_type.317
  43.7 0.7 convert_element_type.314
  44.4 0.7 convert_element_type.311
  45.2 0.7 convert_element_type.307
  45.9 2.6 convert_element_type.308
  49.0 12.2 %all_gather.25 = bf16[3,64,64]{2,1,0:T(8,128)(2,1)S(1)} all-gather(bf16[3,16,64]{2,1,0:T(8,128)(2,1)S(1)} %convert_bitcast_fusion.1), channel_id=1, replica_groups=mesh['dom'=4,'head'=32] {'dom'}, dimensions={1}, use_global_device_ids=true | all-gather | bytes 30720 | tf_op jit(solution)/shard_map/all_gather | solution.py:64
  61.3 11.9 %all_gather.29 = bf16[3,64,256]{2,1,0:T(8,128)(2,1)S(1)} all-gather(bf16[3,16,256]{2,1,0:T(8,128)(2,1)S(1)} %convert_bitcast_fusion), channel_id=1, replica_groups=mesh['dom'=4,'head'=32] {'dom'}, dimensions={1}, use_global_device_ids=true | all-gather | bytes 122880 | tf_op jit(solution)/shard_map/all_gather | solution.py:63
  76.8 0.8 fusion.52
  77.6 0.8 fusion.53
  78.4 0.8 fusion.54
  79.2 0.9 fusion.49
  80.1 0.9 fusion.50
  81.0 0.9 fusion.51
  81.8 1.2 fusion.75
  83.0 4.3 %fusion = f32[384]{0:T(512)S(1)} fusion(bf16[384,8192]{1,0:T(8,128)(2,1)} %all-gather.5.cloned.1.call-done), kind=kLoop, calls=%fused_computation.2 | loop fusion | flops 9436800 | bytes 6292992 | tf_op jit(solution)/shard_map/reduce_sum | solution.py:55
  87.6 2.9 fusion.2
  90.6 2.1 fusion.78
  93.2 0.9 divide_convert_fusion
  94.2 17.6 %fusion.74 = (bf16[8192,1,256]{2,1,0:T(2,128)(2,1)}, bf16[8192,1,256]{2,1,0:T(2,128)(2,1)}) fusion(bf16[8192,2,256]{2,1,0:T(2,128)(2,1)} %param.24), kind=kLoop, calls=%fused_computation.198 | loop fusion | bytes 16777216 | tf_op jit(solution)/shard_map/slice | solution.py:57
  111.9 1.8 negate_multiply_fusion
  114.0 22.3 %all-gather.7.cloned.1.call-done = bf16[384,2048]{0,1:T(8,128)(2,1)} async-done(((bf16[384,64]{0,1:T(8,128)(2,1)}), bf16[384,2048]{0,1:T(8,128)(2,1)}) %all-gather.7.cloned.1.call-update) | async-done | bytes 1572880 | tf_op jit(solution)/shard_map/all_gather | solution.py:67
  136.3 0.9 constant_dynamic-slice_fusion
  137.2 14.9 %all-gather = bf16[1536,256]{0,1:T(8,128)(2,1)S(1)} all-gather(bf16[384,256]{0,1:T(8,128)(2,1)S(1)} %constant_dynamic-slice_fusion), channel_id=2, replica_groups=mesh['dom'=4,'head'=32] {'dom'}, dimensions={0}, use_global_device_ids=true | all-gather | bytes 983040 | tf_op jit(solution)/shard_map/all_gather | solution.py:70
  152.6 1.6 broadcast_multiply_fusion
  168.9 1.2 copy.74
  170.6 7.8 %fusion.4 = f32[384,256]{0,1:T(8,128)S(1)} fusion(bf16[384,8192]{1,0:T(8,128)(2,1)} %copy-done.2, bf16[8192,1,256]{2,1,0:T(2,128)(2,1)} %get-tuple-element.18), kind=kOutput, calls=%fused_computation.9 | convolution fusion | flops 1610612736 | bytes 10878976 | tf_op jit(solution)/shard_map/dot_general | solution.py:58
  178.5 0.8 add_divide_fusion
  179.2 1.2 fusion.32
  180.4 10.9 %reduce-scatter.3.cloned.1.call-done = bf16[1,384,256]{1,2,0:T(8,128)(2,1)} async-done(((bf16[4,384,256]{1,2,0:T(8,128)(2,1)}), bf16[1,384,256]{1,2,0:T(8,128)(2,1)}) %reduce-scatter.3.cloned.1.call-update) | async-done | bytes 196624 | tf_op jit(solution)/shard_map/reduce_scatter | solution.py:80
  191.3 1.0 bitcast_convert_fusion
  192.3 1.0 fusion.9
  193.3 1.1 fusion.8
  194.4 1.0 fusion.7
  195.5 1.1 fusion.6
  196.6 7.7 %multiply_reduce_fusion = (f32[384]{0:T(512)S(1)}, f32[384,256]{0,1:T(8,128)S(1)}) fusion(bf16[384,8192]{1,0:T(8,128)(2,1)} %copy-done.2, bf16[8192,1,256]{2,1,0:T(2,128)(2,1)} %get-tuple-element.17, f32[384,64]{0,1:T(8,128)S(1)} %fusion.6, f32[384,64]{0,1:T(8,128)S(1)} %fusion.7, f32[384,64]{0,1:T(8,128)S(1)} %fusion.8, f32[384,64]{0,1:T(8,128)S(1)} %fusion.9), kind=kOutput, calls=%fused_computation.57 | convolution fusion | flops 1611497088 | bytes 11273728 | tf_op jit(solution)/shard_map/dot_general | solution.py:57
  204.4 24.9 %all_gather.32 = f32[32,4,384]{2,1,0:T(4,128)S(1)} all-gather(f32[1,4,384]{2,1,0:T(4,128)S(1)} %broadcast_select_fusion), channel_id=1, replica_groups=mesh['dom'=4,'head'=32] {'head'}, dimensions={0}, use_global_device_ids=true | all-gather | bytes 202752 | tf_op jit(solution)/shard_map/all_gather | solution.py:105
  229.4 6.7 %convolution_convert_fusion = bf16[384,8192]{1,0:T(8,128)(2,1)} fusion(bf16[256,8192]{1,0:T(8,128)(2,1)} %param.35, f32[384,256]{0,1:T(8,128)S(1)} %get-tuple-element.82, f32[256]{0:T(256)S(1)} %copy-done.41, f32[384]{0:T(512)S(1)} %add_rsqrt_fusion), kind=kOutput, calls=%fused_computation.5 | convolution fusion | flops 1614053376 | bytes 10881536 | tf_op jit(solution)/shard_map/dot_general | solution.py:111
  236.2 84.1 %reduce-scatter.5.cloned.1.call-done = bf16[384,256]{1,0:T(8,128)(2,1)} async-done(((bf16[384,8192]{1,0:T(8,128)(2,1)}), bf16[384,256]{1,0:T(8,128)(2,1)}) %reduce-scatter.5.cloned.1.call-update) | async-done | bytes 196624 | tf_op jit(solution)/shard_map/reduce_scatter | solution.py:112
  (245 shorter events, 25.2 us)
Async XLA Ops:
  6.5 83.9 %copy-start = (bf16[8192,64]{0,1:T(8,128)(2,1)S(1)}, bf16[8192,64]{0,1:T(8,128)(2,1)}, u32[]{:S(2)}) copy-start(bf16[8192,64]{0,1:T(8,128)(2,1)} %param.25) | copy-start | bytes 3145732
  6.5 76.5 %all-gather.5.cloned.1.call-start = ((), (), s32[]{:S(2)}) async-start(), calls=%async_computation.2 | async-start | bytes 6488064 | tf_op jit(solution)/shard_map/all_gather | solution.py:52
  7.3 129.0 %all-gather.7.cloned.1.call-start = ((), (), s32[]{:S(2)}) async-start(), calls=%async_computation.3 | async-start | bytes 1622016 | tf_op jit(solution)/shard_map/all_gather | solution.py:67
  45.9 3.1 copy-start.28
  45.9 15.4 %copy-start.22 = (f32[16,3,256]{2,0,1:T(8,128)S(1)}, f32[16,3,256]{2,0,1:T(8,128)}, u32[]{:S(2)}) copy-start(f32[16,3,256]{2,0,1:T(8,128)} %param.21) | copy-start | bytes 147460
  45.9 29.0 %copy-start.42 = (f32[4]{0:T(128)S(1)}, f32[4]{0:T(128)}, u32[]{:S(2)}) copy-start(f32[4]{0:T(128)} %param.33) | copy-start | bytes 52
  45.9 29.7 %copy-start.55 = (f32[4,64]{1,0:T(4,128)S(1)}, f32[4,64]{1,0:T(4,128)}, u32[]{:S(2)}) copy-start(f32[4,64]{1,0:T(4,128)} %param.29) | copy-start | bytes 3076
  45.9 30.3 %copy-start.45 = (f32[4,256]{1,0:T(4,128)S(1)}, f32[4,256]{1,0:T(4,128)}, u32[]{:S(2)}) copy-start(f32[4,256]{1,0:T(4,128)} %param.27) | copy-start | bytes 12292
  83.0 4.6 %copy-start.4 = (bf16[384,8192]{1,0:T(8,128)(2,1)S(1)}, bf16[384,8192]{1,0:T(8,128)(2,1)}, u32[]{:S(2)}) copy-start(bf16[384,8192]{1,0:T(8,128)(2,1)} %all-gather.5.cloned.1.call-done) | copy-start | bytes 18874372
  90.5 2.7 copy-start.2
  90.5 2.7 copy-start.25
  90.5 2.7 copy-start.26
  90.5 2.7 copy-start.27
  90.5 2.7 copy-start.50
  90.5 2.7 copy-start.51
  94.1 17.7 %copy-start.21 = (bf16[8192,4]{0,1:T(4,128)(2,1)S(1)}, bf16[8192,4]{0,1:T(4,128)(2,1)}, u32[]{:S(2)}) copy-start(bf16[8192,4]{0,1:T(4,128)(2,1)} %param.26) | copy-start | bytes 196612
  94.1 17.7 %copy-start.43 = (f32[4]{0:T(128)S(1)}, f32[4]{0:T(128)}, u32[]{:S(2)}) copy-start(f32[4]{0:T(128)} %param.31) | copy-start | bytes 52
  94.1 17.7 %copy-start.44 = (f32[4]{0:T(128)S(1)}, f32[4]{0:T(128)}, u32[]{:S(2)}) copy-start(f32[4]{0:T(128)} %exp.42) | copy-start | bytes 52
  94.2 97.2 %reduce-scatter.3.cloned.1.call-start = ((), (), s32[]{:S(2)}) async-start(), calls=%async_computation.4 | async-start | bytes 983040 | tf_op jit(solution)/shard_map/reduce_scatter | solution.py:80
  94.2 17.7 %copy-start.3 = (bf16[384,8192]{1,0:T(8,128)(2,1)S(1)}, bf16[384,8192]{1,0:T(8,128)(2,1)}, u32[]{:S(2)}) copy-start(bf16[384,8192]{1,0:T(8,128)(2,1)} %copy-done.2) | copy-start | bytes 18874372
  113.6 38.7 %copy-start.29 = (bf16[4,384]{1,0:T(4,128)(2,1)S(1)}, bf16[4,384]{1,0:T(4,128)(2,1)}, u32[]{:S(2)}) copy-start(bf16[4,384]{1,0:T(4,128)(2,1)} %convert_element_type.341) | copy-start | bytes 9220
  113.7 38.7 %copy-start.30 = (bf16[4,384]{1,0:T(4,128)(2,1)S(1)}, bf16[4,384]{1,0:T(4,128)(2,1)}, u32[]{:S(2)}) copy-start(bf16[4,384]{1,0:T(4,128)(2,1)} %convert_element_type.338) | copy-start | bytes 9220
  113.7 38.7 %copy-start.31 = (bf16[4,384]{1,0:T(4,128)(2,1)S(1)}, bf16[4,384]{1,0:T(4,128)(2,1)}, u32[]{:S(2)}) copy-start(bf16[4,384]{1,0:T(4,128)(2,1)} %convert_element_type.335) | copy-start | bytes 9220
  113.7 38.8 %copy-start.32 = (bf16[4,384]{1,0:T(4,128)(2,1)S(1)}, bf16[4,384]{1,0:T(4,128)(2,1)}, u32[]{:S(2)}) copy-start(bf16[4,384]{1,0:T(4,128)(2,1)} %convert_element_type.332) | copy-start | bytes 9220
  113.7 38.8 %copy-start.33 = (bf16[4,384]{1,0:T(4,128)(2,1)S(1)}, bf16[4,384]{1,0:T(4,128)(2,1)}, u32[]{:S(2)}) copy-start(bf16[4,384]{1,0:T(4,128)(2,1)} %convert_element_type.329) | copy-start | bytes 9220
  113.7 38.8 %copy-start.34 = (bf16[4,384]{1,0:T(4,128)(2,1)S(1)}, bf16[4,384]{1,0:T(4,128)(2,1)}, u32[]{:S(2)}) copy-start(bf16[4,384]{1,0:T(4,128)(2,1)} %convert_element_type.326) | copy-start | bytes 9220
  113.7 38.8 %copy-start.35 = (bf16[4,384]{1,0:T(4,128)(2,1)S(1)}, bf16[4,384]{1,0:T(4,128)(2,1)}, u32[]{:S(2)}) copy-start(bf16[4,384]{1,0:T(4,128)(2,1)} %convert_element_type.323) | copy-start | bytes 9220
  113.7 38.8 %copy-start.36 = (bf16[4,384]{1,0:T(4,128)(2,1)S(1)}, bf16[4,384]{1,0:T(4,128)(2,1)}, u32[]{:S(2)}) copy-start(bf16[4,384]{1,0:T(4,128)(2,1)} %convert_element_type.320) | copy-start | bytes 9220
  113.7 38.8 %copy-start.37 = (bf16[4,384]{1,0:T(4,128)(2,1)S(1)}, bf16[4,384]{1,0:T(4,128)(2,1)}, u32[]{:S(2)}) copy-start(bf16[4,384]{1,0:T(4,128)(2,1)} %convert_element_type.317) | copy-start | bytes 9220
  113.8 38.8 %copy-start.38 = (bf16[4,384]{1,0:T(4,128)(2,1)S(1)}, bf16[4,384]{1,0:T(4,128)(2,1)}, u32[]{:S(2)}) copy-start(bf16[4,384]{1,0:T(4,128)(2,1)} %convert_element_type.314) | copy-start | bytes 9220
  113.8 38.8 %copy-start.39 = (bf16[4,384]{1,0:T(4,128)(2,1)S(1)}, bf16[4,384]{1,0:T(4,128)(2,1)}, u32[]{:S(2)}) copy-start(bf16[4,384]{1,0:T(4,128)(2,1)} %convert_element_type.311) | copy-start | bytes 9220
  113.9 38.7 %copy-start.40 = (bf16[4,384]{1,0:T(4,128)(2,1)S(1)}, bf16[4,384]{1,0:T(4,128)(2,1)}, u32[]{:S(2)}) copy-start(bf16[4,384]{1,0:T(4,128)(2,1)} %convert_element_type.307) | copy-start | bytes 9220
  114.0 40.3 %copy-start.23 = (f32[384,4]{0,1:T(4,128)}, f32[384,4]{0,1:T(4,128)S(1)}, u32[]{:S(2)}) copy-start(f32[384,4]{0,1:T(4,128)S(1)} %pad_add_fusion.2) | copy-start | bytes 18436
  170.1 150.2 %reduce-scatter.5.cloned.1.call-start = ((), (), s32[]{:S(2)}) async-start(), calls=%async_computation.5 | async-start | bytes 6488064 | tf_op jit(solution)/shard_map/reduce_scatter | solution.py:112
  170.5 7.9 %copy-start.18 = (f32[16,256]{0,1:T(8,128)S(1)}, f32[16,256]{0,1:T(8,128)}, u32[]{:S(2)}) copy-start(f32[16,256]{0,1:T(8,128)} %fusion.49) | copy-start | bytes 49156
  170.5 7.9 %copy-start.19 = (f32[16,256]{0,1:T(8,128)S(1)}, f32[16,256]{0,1:T(8,128)}, u32[]{:S(2)}) copy-start(f32[16,256]{0,1:T(8,128)} %fusion.50) | copy-start | bytes 49156
  170.5 7.9 %copy-start.20 = (f32[16,256]{0,1:T(8,128)S(1)}, f32[16,256]{0,1:T(8,128)}, u32[]{:S(2)}) copy-start(f32[16,256]{0,1:T(8,128)} %fusion.51) | copy-start | bytes 49156
  170.5 7.9 %copy-start.46 = (f32[1,256]{1,0:T(1,128)S(1)}, f32[1,256]{1,0:T(1,128)}, u32[]{:S(2)}) copy-start(f32[1,256]{1,0:T(1,128)} %get-tuple-element.51) | copy-start | bytes 3076
  170.5 7.9 %copy-start.47 = (f32[1,256]{1,0:T(1,128)S(1)}, f32[1,256]{1,0:T(1,128)}, u32[]{:S(2)}) copy-start(f32[1,256]{1,0:T(1,128)} %get-tuple-element.52) | copy-start | bytes 3076
  170.5 7.9 %copy-start.48 = (f32[1,256]{1,0:T(1,128)S(1)}, f32[1,256]{1,0:T(1,128)}, u32[]{:S(2)}) copy-start(f32[1,256]{1,0:T(1,128)} %get-tuple-element.53) | copy-start | bytes 3076
  170.5 7.9 %copy-start.49 = (f32[1,256]{1,0:T(1,128)S(1)}, f32[1,256]{1,0:T(1,128)}, u32[]{:S(2)}) copy-start(f32[1,256]{1,0:T(1,128)} %get-tuple-element.54) | copy-start | bytes 3076
  170.5 7.9 %copy-start.58 = (f32[256]{0:T(256)S(1)}, f32[256]{0:T(256)}, u32[]{:S(2)}) copy-start(f32[256]{0:T(256)} %param.28) | copy-start | bytes 3076
  178.3 13.9 %copy-start.56 = (s32[384]{0:T(512)S(1)}, s32[384]{0:T(512)}, u32[]{:S(2)}) copy-start(s32[384]{0:T(512)} %get-tuple-element.83) | copy-start | bytes 4612
  178.4 13.9 %copy-start.57 = (s32[384]{0:T(512)S(1)}, s32[384]{0:T(512)}, u32[]{:S(2)}) copy-start(s32[384]{0:T(512)} %get-tuple-element.84) | copy-start | bytes 4612
  178.4 13.9 %copy-start.61 = (pred[384]{0:T(512)(128)(4,1)S(1)}, pred[384]{0:T(512)(128)(4,1)}, u32[]{:S(2)}) copy-start(pred[384]{0:T(512)(128)(4,1)} %fusion.64) | copy-start | bytes 1156
  196.6 7.7 %copy-start.54 = (pred[4]{0:T(512)(128)(4,1)S(1)}, pred[4]{0:T(512)(128)(4,1)}, u32[]{:S(2)}) copy-start(pred[4]{0:T(512)(128)(4,1)} %iota_compare_fusion.8) | copy-start | bytes 16
  196.6 32.8 %copy-start.41 = (f32[256]{0:T(256)S(1)}, f32[256]{0:T(256)}, u32[]{:S(2)}) copy-start(f32[256]{0:T(256)} %param.34) | copy-start | bytes 3076
  236.2 84.1 %copy-start.1 = (bf16[8192,64]{0,1:T(8,128)(2,1)S(1)}, bf16[8192,64]{0,1:T(8,128)(2,1)}, u32[]{:S(2)}) copy-start(bf16[8192,64]{0,1:T(8,128)(2,1)} %param.25) | copy-start | bytes 3145732
  (19 other events, 25.5 us)
Sparse Core Ops, SparseCore 0:
  9.5 56.9 all-gather.4
  94.2 41.9 all-gather.6
  170.2 21.0 reduce-scatter.2
  236.3 83.9 reduce-scatter.4
